TPU v7x, 128 devices: a whole 4x4x4 slice. The times are simulated.
128 devices in a mesh: dp: 16 (over x, y_hi, core), seq: 8 (over y_lo, z).
Axes of the slice: x: 4, y: 4 (y_hi: 2, y_lo: 2; y = y_hi * 2 + y_lo), z: 4, core: 2. Of those that a mesh axis runs over, the one named last changes fastest.
Arguments:
- grad_out: bfloat16 [16384, 4096], P(('dp', 'seq')), may hold values from -6 to 6
- moe_input: bfloat16 [16384, 4096], P(('dp', 'seq')), may hold values from -900 to 900
- router_weight: bfloat16 [4096, 128], replicated, may hold values from -0.09375 to 0.09375
- routes: int32 [16384, 8], P(('dp', 'seq')), may hold values from 0 to 127, as said below
- gate_saved: bfloat16 [128, 128, 12, 768], P(('dp', 'seq')), may hold values from -8 to 8
- up_saved: bfloat16 [128, 128, 12, 768], P(('dp', 'seq')), may hold values from -6 to 6
- expert_gate: bfloat16 [128, 4096, 768], P(('dp', 'seq')), may hold values from -0.09375 to 0.09375
- expert_up: bfloat16 [128, 4096, 768], P(('dp', 'seq')), may hold values from -0.09375 to 0.09375
- expert_down: bfloat16 [128, 768, 4096], P(('dp', 'seq')), may hold values from -0.21875 to 0.21875
Outputs:
- input_grad: bfloat16 [16384, 4096], P(('dp', 'seq'))
- router_grad: float32 [128, 4096], P(('dp', 'seq'))
Inputs may be any that keep to these rules, and one draw needn't show every extreme that they name: `routes`: among the picks of one block of 128 tokens, each expert is named at most 12 times, and some expert is named exactly 12 times in every block; the 8 picks of a token differ.
All inputs are finite; a program needn't handle non-finite values.
Results may differ from a plain program's by a relative error of at most 0.014.
Values may be sent and summed in bfloat16 or wider, within the bound.
A program may use at most 192 MiB of HBM per device.

v0:
```python
import jax
import jax.numpy as jnp
from jax import lax
from jax.sharding import PartitionSpec as P


def expert_backward(rows, weights, gate_pre, up_pre, gate_weight, up_weight, down_weight):
    projected = lax.dot_general(
        rows, down_weight, (((1,), (1,)), ((), ())), preferred_element_type=jnp.float32
    )
    gate_value = gate_pre.astype(jnp.float32)
    up_value = up_pre.astype(jnp.float32)
    sigmoid_gate = jax.nn.sigmoid(gate_value)
    activated = gate_value * sigmoid_gate
    inner_sum = jnp.sum(projected * activated * up_value, axis=1).astype(jnp.bfloat16)
    scaled_grad = weights.astype(jnp.float32)[:, None] * projected
    gate_grad = (
        scaled_grad * up_value * sigmoid_gate * (1.0 + gate_value * (1.0 - sigmoid_gate))
    ).astype(jnp.bfloat16)
    up_grad = (scaled_grad * activated).astype(jnp.bfloat16)
    summed = lax.dot_general(
        gate_grad, gate_weight, (((1,), (1,)), ((), ())), preferred_element_type=jnp.float32
    )
    summed = summed + lax.dot_general(
        up_grad, up_weight, (((1,), (1,)), ((), ())), preferred_element_type=jnp.float32
    )
    return (summed.astype(jnp.bfloat16), inner_sum)


def shards(
    grad_out,
    moe_input,
    router_weight,
    routes,
    gate_saved,
    up_saved,
    expert_gate,
    expert_up,
    expert_down,
):
    tok_rows, model_width = grad_out.shape
    top_picks = routes.shape[1]
    experts = router_weight.shape[1]
    sources = gate_saved.shape[1]
    capacity = gate_saved.shape[2]
    hidden = gate_saved.shape[3]
    logits = jnp.dot(moe_input, router_weight, preferred_element_type=jnp.float32)
    expert_ids = jnp.arange(experts, dtype=jnp.int32)
    picked = routes[:, :, None] == expert_ids[None, None, :]
    chosen = jnp.sum(jnp.where(picked, logits[:, None, :], jnp.float32(0.0)), axis=-1)
    highest = jnp.max(chosen, axis=1, keepdims=True)
    raised = jnp.exp(chosen - highest)
    combine = raised / jnp.sum(raised, axis=1, keepdims=True)
    combine_sent = combine.astype(jnp.bfloat16)
    targets = routes.reshape(-1)
    onehot = (targets[:, None] == expert_ids[None, :]).astype(jnp.int32)
    ranking = jnp.cumsum(onehot, axis=0) - 1
    slot_index = jnp.sum(ranking * onehot, axis=1)
    position = targets * capacity + slot_index
    token_of = jnp.arange(tok_rows * top_picks, dtype=jnp.int32) // top_picks
    lookup = jnp.full((experts * capacity,), tok_rows, jnp.int32).at[position].set(token_of)
    padded = jnp.concatenate([grad_out, jnp.zeros((1, model_width), jnp.bfloat16)], axis=0)
    outgoing = padded[lookup].reshape(experts, capacity, model_width)
    weight_slots = (
        jnp.zeros((experts * capacity,), jnp.bfloat16).at[position].set(combine_sent.reshape(-1))
    )
    weight_slots = weight_slots.reshape(experts, capacity)
    rows_in, weights_in = (
        lax.all_to_all(outgoing, ("dp", "seq"), split_axis=0, concat_axis=0, tiled=True),
        lax.all_to_all(weight_slots, ("dp", "seq"), split_axis=0, concat_axis=0, tiled=True),
    )
    summed, inner_sum = expert_backward(
        rows_in.reshape(sources * capacity, model_width),
        weights_in.reshape(sources * capacity),
        gate_saved.reshape(sources * capacity, hidden),
        up_saved.reshape(sources * capacity, hidden),
        expert_gate[0],
        expert_up[0],
        expert_down[0],
    )
    arrived, scores = (
        lax.all_to_all(
            summed.reshape(sources, capacity, model_width),
            ("dp", "seq"),
            split_axis=0,
            concat_axis=0,
            tiled=True,
        ),
        lax.all_to_all(
            inner_sum.reshape(sources, capacity),
            ("dp", "seq"),
            split_axis=0,
            concat_axis=0,
            tiled=True,
        ),
    )
    pick_rows = arrived.reshape(experts * capacity, model_width)[position]
    moe_part = jnp.sum(
        pick_rows.reshape(tok_rows, top_picks, model_width).astype(jnp.float32), axis=1
    )
    pick_score = (
        scores.reshape(experts * capacity)[position]
        .reshape(tok_rows, top_picks)
        .astype(jnp.float32)
    )
    chosen_grad = combine * (pick_score - jnp.sum(combine * pick_score, axis=1, keepdims=True))
    logit_grad = jnp.sum(
        jnp.where(picked, chosen_grad[:, :, None], jnp.float32(0.0)), axis=1
    ).astype(jnp.bfloat16)
    routed = lax.dot_general(
        logit_grad, router_weight, (((1,), (1,)), ((), ())), preferred_element_type=jnp.float32
    )
    input_grad = (moe_part + routed).astype(jnp.bfloat16)
    router_terms = lax.dot_general(
        logit_grad, moe_input, (((0,), (0,)), ((), ())), preferred_element_type=jnp.float32
    )
    router_grad = lax.psum_scatter(router_terms, ("dp", "seq"), scatter_dimension=0, tiled=True)
    return (input_grad, router_grad)


def solution(mesh):
    placed = (
        P(("dp", "seq"), None),
        P(("dp", "seq"), None),
        P(),
        P(("dp", "seq"), None),
        P(("dp", "seq"), None, None, None),
        P(("dp", "seq"), None, None, None),
        P(("dp", "seq"), None, None),
        P(("dp", "seq"), None, None),
        P(("dp", "seq"), None, None),
    )
    return jax.shard_map(
        shards,
        mesh=mesh,
        in_specs=placed,
        out_specs=(P(("dp", "seq"), None), P(("dp", "seq"), None)),
        check_vma=False,
    )
```

profile of v0, /device:TPU:1, one launch (start us, length us, event | category | flops | bytes accessed | tf_op | source)
XLA Modules:
  0.0 826.0 jit_solution(15666666246300777948)
XLA Ops:
  7.2 0.8 broadcast_multiply_fusion
  8.0 0.8 copy.43
  10.0 4.3 scatter_custom_fusion.1
  14.4 1.3 concatenate.3
  15.7 9.5 %gather_fusion = bf16[1536,4096]{1,0:T(8,128)(2,1)} fusion(bf16[129,4096]{1,0:T(8,128)(2,1)S(1)} %concatenate.3, s32[2048]{0:T(1024)S(1)} %pad_clamp_fusion), kind=kCustom, calls=%fused_computation | custom fusion | bytes 25171968 | tf_op jit(solution)/shard_map/gather | solution.py:63
  25.3 17.9 %reshape.174 = bf16[128,12,4096]{2,1,0:T(8,128)(2,1)} reshape(bf16[1536,4096]{1,0:T(8,128)(2,1)} %gather_fusion) | data formatting | bytes 25165824 | tf_op jit(solution)/shard_map/reshape | solution.py:63
  43.1 12.3 %all-to-all-start.1 = ((bf16[128,12,4096]{2,1,0:T(8,128)(2,1)}), bf16[128,12,4096]{2,1,0:T(8,128)(2,1)}, u32[]{:S(2)}, u32[]{:S(2)}) async-start(bf16[128,12,4096]{2,1,0:T(8,128)(2,1)} %reshape.174), calls=%async_computation.1 | async-start | bytes 33554432 | tf_op jit(solution)/shard_map/all_to_all | solution.py:69
  55.5 4.1 copy.51
  59.6 6.7 reshape.181
  66.2 6.2 copy.52
  72.4 4.0 copy.49
  76.4 6.7 reshape.180
  83.1 6.2 copy.50
  90.2 189.0 %all-to-all-done.1 = bf16[128,12,4096]{2,1,0:T(8,128)(2,1)} async-done(((bf16[128,12,4096]{2,1,0:T(8,128)(2,1)}), bf16[128,12,4096]{2,1,0:T(8,128)(2,1)}, u32[]{:S(2)}, u32[]{:S(2)}) %all-to-all-start.1) | async-done | bytes 12582944 | tf_op jit(solution)/shard_map/all_to_all | solution.py:69
  279.3 18.1 %reshape.175 = bf16[1536,4096]{1,0:T(8,128)(2,1)} reshape(bf16[128,12,4096]{2,1,0:T(8,128)(2,1)} %all-to-all-done.1) | data formatting | bytes 25165824 | tf_op jit(solution)/shard_map/reshape | solution.py:73
  297.3 18.8 %multiply_reduce_fusion = (bf16[1536]{0:T(1024)(128)(2,1)S(1)}, f32[1536,768]{0,1:T(8,128)}) fusion(f32[1536,768]{0,1:T(8,128)} %copy.50, f32[1536,768]{0,1:T(8,128)} %copy.52, bf16[1536,4096]{1,0:T(8,128)(2,1)} %reshape.175, bf16[1,768,4096]{2,1,0:T(8,128)(2,1)} %param.17), kind=kOutput, calls=%fused_computation.14 | convolution fusion | flops 9671931904 | bytes 33033216 | tf_op jit(solution)/shard_map/dot_general | solution.py:8
  316.9 10.3 %all-to-all-start.3 = ((bf16[128,1,12]{2,1,0:T(2,128)(2,1)}), bf16[128,1,12]{2,1,0:T(2,128)(2,1)S(1)}, u32[]{:S(2)}, u32[]{:S(2)}) async-start(bf16[128,1,12]{2,1,0:T(2,128)(2,1)} %convert_element_type.104), calls=%async_computation.3 | async-start | bytes 131072 | tf_op jit(solution)/shard_map/all_to_all | solution.py:89
  327.4 9.6 %all-to-all-done.3 = bf16[128,1,12]{2,1,0:T(2,128)(2,1)S(1)} async-done(((bf16[128,1,12]{2,1,0:T(2,128)(2,1)}), bf16[128,1,12]{2,1,0:T(2,128)(2,1)S(1)}, u32[]{:S(2)}, u32[]{:S(2)}) %all-to-all-start.3) | async-done | bytes 3104 | tf_op jit(solution)/shard_map/all_to_all | solution.py:89
  337.3 6.8 gather_fusion.2
  344.7 7.6 scatter_custom_fusion
  352.4 13.9 %all_to_all.26 = bf16[128,1,12]{2,1,0:T(2,128)(2,1)S(1)} all-to-all(bf16[128,1,12]{2,1,0:T(2,128)(2,1)S(1)} %all_to_all.21), channel_id=1, replica_groups=mesh['dp'=16,'seq'=8] {'dp','seq'}, dimensions={0} | all-to-all | bytes 6144 | tf_op jit(solution)/shard_map/all_to_all | solution.py:70
  366.5 24.0 %fusion.1 = f32[1536,4096]{1,0:T(8,128)} fusion(bf16[1,4096,768]{2,1,0:T(8,128)(2,1)} %param.15, f32[1536,768]{0,1:T(8,128)} %copy.52, f32[1536,768]{0,1:T(8,128)} %copy.50, f32[1536,768]{0,1:T(8,128)} %get-tuple-element.5, f32[1536]{0:T(1024)S(1)} %reshape.179), kind=kOutput, calls=%fused_computation.8 | convolution fusion | flops 9676652544 | bytes 45619200 | tf_op jit(solution)/shard_map/dot_general | solution.py:21
  390.5 23.1 %add_convert_fusion = bf16[1536,4096]{1,0:T(8,128)(2,1)} fusion(f32[1536,4096]{1,0:T(8,128)} %fusion.1, bf16[1,4096,768]{2,1,0:T(8,128)(2,1)} %param.16, f32[1536,768]{0,1:T(8,128)} %get-tuple-element.5, f32[1536]{0:T(1024)S(1)} %reshape.179, f32[1536,768]{0,1:T(8,128)} %copy.52), kind=kOutput, calls=%fused_computation.5 | convolution fusion | flops 9684516864 | bytes 53483520 | tf_op jit(solution)/shard_map/dot_general | solution.py:24
  413.7 17.9 %reshape.176 = bf16[128,12,4096]{2,1,0:T(8,128)(2,1)} reshape(bf16[1536,4096]{1,0:T(8,128)(2,1)} %add_convert_fusion) | data formatting | bytes 25165824 | tf_op jit(solution)/shard_map/reshape | solution.py:83
  431.6 5.2 all-to-all-start.2
  437.4 1.8 fusion.31
  439.2 327.1 %all-reduce.4.cloned.1.call-done = f32[128,4096]{1,0:T(8,128)} async-done(((f32[128,4096]{1,0:T(8,128)}), f32[128,4096]{1,0:T(8,128)}) %all-reduce.4.cloned.1.call-update) | async-done | bytes 2097168
  766.4 1.5 constant_dynamic-slice_fusion
  767.9 18.2 %reshape.177 = bf16[1536,4096]{1,0:T(8,128)(2,1)} reshape(bf16[128,12,4096]{2,1,0:T(8,128)(2,1)} %all-to-all-done.2) | data formatting | bytes 25165824 | tf_op jit(solution)/shard_map/reshape | solution.py:97
  786.1 21.3 %gather_fusion.1 = bf16[1024,4096]{1,0:T(8,128)(2,1)} fusion(bf16[1536,4096]{1,0:T(8,128)(2,1)} %reshape.177, s32[1024]{0:T(1024)S(1)} %broadcast_clamp_fusion), kind=kCustom, calls=%fused_computation.1 | custom fusion | bytes 16781312 | tf_op jit(solution)/shard_map/gather | solution.py:97
  807.3 9.1 %convert_reduce_fusion = f32[128,4096]{1,0:T(8,128)S(1)} fusion(bf16[1024,4096]{1,0:T(8,128)(2,1)} %gather_fusion.1), kind=kLoop, calls=%fused_computation.6 | loop fusion | flops 7864320 | bytes 10485760 | tf_op jit(solution)/shard_map/reduce_sum | solution.py:98
  816.4 2.6 fusion.5
  (43 shorter events, 4.9 us)
Async XLA Ops:
  7.2 82.1 %copy-start = (bf16[128,4096]{1,0:T(8,128)(2,1)S(1)}, bf16[128,4096]{1,0:T(8,128)(2,1)}, u32[]{:S(2)}) copy-start(bf16[128,4096]{1,0:T(8,128)(2,1)} %param.10) | copy-start | bytes 3145732
  43.1 12.3 %copy-start.2 = (bf16[1,128,12,768]{3,1,2,0:T(8,128)(2,1)S(1)}, bf16[1,128,12,768]{3,1,2,0:T(8,128)(2,1)}, u32[]{:S(2)}) copy-start(bf16[1,128,12,768]{3,1,2,0:T(8,128)(2,1)} %param.13) | copy-start | bytes 7077892
  43.1 236.1 %all-to-all-start.1 = ((bf16[128,12,4096]{2,1,0:T(8,128)(2,1)}), bf16[128,12,4096]{2,1,0:T(8,128)(2,1)}, u32[]{:S(2)}, u32[]{:S(2)}) async-start(bf16[128,12,4096]{2,1,0:T(8,128)(2,1)} %reshape.174), calls=%async_computation.1 | async-start | bytes 33554432 | tf_op jit(solution)/shard_map/all_to_all | solution.py:69
  66.2 6.2 copy-start.3
  83.1 6.2 copy-start.1
  316.9 20.1 %all-to-all-start.3 = ((bf16[128,1,12]{2,1,0:T(2,128)(2,1)}), bf16[128,1,12]{2,1,0:T(2,128)(2,1)S(1)}, u32[]{:S(2)}, u32[]{:S(2)}) async-start(bf16[128,1,12]{2,1,0:T(2,128)(2,1)} %convert_element_type.104), calls=%async_computation.3 | async-start | bytes 131072 | tf_op jit(solution)/shard_map/all_to_all | solution.py:89
  431.6 336.3 %all-to-all-start.2 = ((bf16[128,12,4096]{2,1,0:T(8,128)(2,1)}), bf16[128,12,4096]{2,1,0:T(8,128)(2,1)}, u32[]{:S(2)}, u32[]{:S(2)}) async-start(bf16[128,12,4096]{2,1,0:T(8,128)(2,1)} %reshape.176), calls=%async_computation.2 | async-start | bytes 33554432 | tf_op jit(solution)/shard_map/all_to_all | solution.py:82
  436.8 329.6 %all-reduce.4.cloned.1.call-start = ((), (), s32[]{:S(2)}) async-start(), calls=%async_computation.4 | async-start | bytes 4194304
Sparse Core Ops, SparseCore 0:
  442.5 323.8 all-reduce.3
where the time goes:
time: 838 us; the launch traced here: 826 us
  waiting for transfers between devices  526 us (63%)
  local copies, waits for them, and re-layouts  161 us (19%)
  matrix products  70.8 us (8%)
  starting transfers between devices  28.1 us (3%)
  between operations  14.4 us (2%)
  blocking collectives  13.9 us (2%)
  other arithmetic  12.2 us (1%)
    unnamed x2, waiting for transfers between devices  327 us
    all_to_all x1, waiting for transfers between devices, shards(): lax.all_to_all(outgoing, ('dp', 'seq'), split_axis=0, concat_axis=0, tile...  189 us
    dot_general x1, matrix products, expert_backward(): lax.dot_general(gate_grad, gate_weight, (((1,), (1,)), ((), ())), preferr...  24 us
    dot_general x1, matrix products, expert_backward(): lax.dot_general(up_grad, up_weight, (((1,), (1,)), ((), ())), preferred_e...  23.1 us
    gather x1, local copies, waits for them, and re-layouts, shards(): pick_rows = arrived.reshape(experts * capacity, model_width)[position]  21.3 us
    dot_general x1, matrix products, expert_backward(): lax.dot_general(rows, down_weight, (((1,), (1,)), ((), ())), preferred_el...  18.8 us
    reshape x1, local copies, waits for them, and re-layouts, shards(): pick_rows = arrived.reshape(experts * capacity, model_width)[position]  18.2 us
    reshape x1, local copies, waits for them, and re-layouts, shards(): rows_in.reshape(sources * capacity, model_width)  18.1 us
  transfers between devices with their start and end apart: 4, of which 3 were waited for; matrix products, arithmetic and copies ran while one was open for 5% of the time, Pallas kernels for 0%

commit v1 on v0

v1 whole, which is shorter than its diff:
```python
import jax
import jax.numpy as jnp
from jax import lax
from jax.experimental import pallas as pl
from jax.experimental.pallas import tpu as pltpu
from jax.sharding import PartitionSpec as P

MESH = pl.DeviceIdType.MESH
F32, BF16 = jnp.float32, jnp.bfloat16
COL = 1024
LAST = 3 * COL
HID = 768
SLOTS = 12


def nt(a, b):
    return lax.dot_general(a, b, (((1,), (1,)), ((), ())), preferred_element_type=F32)


def nn(a, b):
    return lax.dot_general(a, b, (((1,), (0,)), ((), ())), preferred_element_type=F32)


def iota(shape, dim):
    return lax.broadcasted_iota(jnp.int32, shape, dim)


def onehot(cond):
    return jnp.where(cond, 1.0, 0.0).astype(BF16)


def device(x, y, z, c):
    return (x * 4 + (y // 2) * 2 + c, (y % 2) * 4 + z)


def expert_id(x, y, z, c):
    return x * 32 + (y // 2) * 16 + c * 8 + (y % 2) * 4 + z


def plane_member(part, ahead, b, here, c):
    x, y, z = here
    return (
        (x, (y + ahead) % 4, b, c),
        (b, y, (z + ahead) % 4, c),
        ((x + ahead) % 4, b, z, c),
    )[part]


def line_member(part, position, here, c):
    x, y, z = here
    return ((position, y, z, c), (x, position, z, c), (x, y, position, c))[part]


def kernel(
    x_ref, h_ref, rw_ref, routes_ref, gs_hbm, us_hbm, wg_hbm, wu_hbm, wd_hbm,
    out_ref, router_ref, back_hbm,
    gathered, meta, staged, landed, wd, wg, wu, gs_buf, us_buf,
    expand, combine_ref, slots_ref, score_rows, score_send, score_plane, score_line,
    score_all, terms_in, rows_out, rows_in,
    w_sem, gs_sem, ax_send, ax_recv, am_send, am_recv, own_sem,
    d_send, d_recv, r_send, r_recv, sp_send, sp_recv, sl_send, sl_recv,
    t_send, t_recv, q_send, q_recv, load_sem, p_send, p_recv,
):
    dp, seq = lax.axis_index("dp"), lax.axis_index("seq")
    x, c, z = dp // 4, dp % 2, seq % 4
    yh, yl = (dp // 2) % 2, seq // 4
    y = yh * 2 + yl
    here = (x, y, z)
    second = (z, x, y)
    sign = 1 - 2 * c
    my_plane = (dp % 4) * 8 + seq

    def weight_copies():
        copies = []
        for p in range(4):
            columns = pl.ds(p * COL, COL)
            copies.append(pltpu.make_async_copy(wd_hbm.at[:, columns], wd.at[p], w_sem.at[p]))
        copies.append(pltpu.make_async_copy(wg_hbm, wg, w_sem.at[4]))
        copies.append(pltpu.make_async_copy(wu_hbm, wu, w_sem.at[5]))
        return copies

    for copy in weight_copies():
        copy.start()

    barrier = pltpu.get_barrier_semaphore()

    def greet(target):
        pl.semaphore_signal(barrier, inc=1, device_id=device(*target), device_id_type=MESH)

    def greet_x(k, carry):
        greet((x, (y + k // 8) % 4, (z + (k // 2) % 4) % 4, (c + k % 2) % 2))
        return carry

    def greet_y(k, carry):
        greet(((x + 1 + k // 8) % 4, y, (z + (k // 2) % 4) % 4, (c + k % 2) % 2))
        return carry

    def greet_z(k, carry):
        greet(((x + 1 + k // 6) % 4, (y + 1 + (k // 2) % 3) % 4, z, (c + k % 2) % 2))
        return carry

    lax.fori_loop(1, 32, greet_x, 0)
    lax.fori_loop(0, 24, greet_y, 0)
    lax.fori_loop(0, 18, greet_z, 0)

    square = (128, 128)
    picked_t = jnp.zeros(square, F32)
    for k in range(8):
        picked_t = picked_t + jnp.where(routes_ref[k : k + 1, :] == iota(square, 0), 1.0, 0.0)
    picked_t = picked_t.astype(BF16)
    picked = nt(onehot(iota(square, 0) == iota(square, 1)), picked_t) > 0.5
    earlier = nt(onehot(iota(square, 1) < iota(square, 0)), picked_t)
    slots = jnp.where(picked, earlier, -1.0)
    slots_ref[...] = slots

    pl.semaphore_wait(barrier, 73)

    def token_copies(part, step):
        position = (here[part] + step) % 4
        to = device(*line_member(part, position, here, c))
        return [
            pltpu.make_async_remote_copy(
                src_ref=x_ref.at[:, pl.ds(first, COL)],
                dst_ref=gathered.at[part, here[part], pl.ds(128 * n, 128)],
                send_sem=ax_send.at[part, step, n],
                recv_sem=ax_recv.at[part, here[part], n],
                device_id=to,
                device_id_type=MESH,
            )
            for n, first in enumerate((part * COL, LAST))
        ]

    for step in (1, 3, 2):
        for part in range(3):
            for copy in token_copies(part, step):
                copy.start()

    logits = nn(h_ref[...], rw_ref[...])
    highest = jnp.max(jnp.where(picked, logits, -jnp.inf), axis=1, keepdims=True)
    raised = jnp.where(picked, jnp.exp(jnp.where(picked, logits, highest) - highest), 0.0)
    combine = raised / jnp.sum(raised, axis=1, keepdims=True)
    combine_ref[...] = combine
    for part in range(3):
        meta[part, here[part], 0:128, :] = slots.astype(BF16)
        meta[part, here[part], 128:256, :] = combine.astype(BF16)

    def meta_copy(part, step):
        position = (here[part] + step) % 4
        return pltpu.make_async_remote_copy(
            src_ref=meta.at[part, here[part]],
            dst_ref=meta.at[part, here[part]],
            send_sem=am_send.at[part, step],
            recv_sem=am_recv.at[part, here[part]],
            device_id=device(*line_member(part, position, here, c)),
            device_id_type=MESH,
        )

    for step in (1, 3, 2):
        for part in range(3):
            meta_copy(part, step).start()

    for part in range(3):
        gathered[part, here[part], 0:128, :] = x_ref[:, part * COL : (part + 1) * COL]
        gathered[part, here[part], 128:256, :] = x_ref[:, LAST:]

    row, lane = iota((512, 128), 0), iota((512, 128), 1)
    ahead = sign * (row // 128) + 4
    core = (c + (row // 64) % 2) % 2
    b = (row // 16) % 4
    for part in range(3):
        owner = expert_id(*plane_member(part, ahead, b, here, core))
        expand[part] = onehot(owner == lane)

    def message(buffer, part, a, dc, b):
        if part == 1:
            return buffer.at[1, a, :, dc, :, b]
        return buffer.at[part, a, dc, b // 2, b % 2]

    def dispatch_copy(part, k):
        a, dc, b = k // 8, (k // 4) % 2, (second[part] + k % 4) % 4
        to = plane_member(part, sign * a + 4, b, here, (c + dc) % 2)
        landing = (
            landed.at[0, :, yh, c, yl, z],
            landed.at[1, x, :, c, :, z],
            landed.at[2, x, yh, c, yl],
        )[part]
        return pltpu.make_async_remote_copy(
            src_ref=message(staged, part, a, dc, b),
            dst_ref=landing,
            send_sem=d_send.at[part, k],
            recv_sem=d_recv.at[part, a * 8 + dc * 4 + second[part]],
            device_id=device(*to),
            device_id_type=MESH,
        )

    def own_copy(part):
        landing = (
            landed.at[0, :, yh, c, yl, z],
            landed.at[1, x, :, c, :, z],
            landed.at[2, x, yh, c, yl],
        )[part]
        return pltpu.make_async_copy(
            message(staged, part, 0, 0, second[part]), landing, own_sem.at[part]
        )

    slot_of_row = iota((512, 128), 0) % 16

    def wait_line(part):
        for step in (1, 2, 3):
            position = (here[part] + step) % 4
            for n in range(2):
                pltpu.make_async_remote_copy(
                    src_ref=gathered.at[part, position, pl.ds(128 * n, 128)],
                    dst_ref=gathered.at[part, position, pl.ds(128 * n, 128)],
                    send_sem=ax_send.at[part, step, n],
                    recv_sem=ax_recv.at[part, position, n],
                    device_id=device(*line_member(part, position, here, c)),
                    device_id_type=MESH,
                ).wait_recv()
            pltpu.make_async_remote_copy(
                src_ref=meta.at[part, position],
                dst_ref=meta.at[part, position],
                send_sem=am_send.at[part, step],
                recv_sem=am_recv.at[part, position],
                device_id=device(*line_member(part, position, here, c)),
                device_id_type=MESH,
            ).wait_recv()

    def extra_slot(part):
        return jnp.where(slot_of_row >= SLOTS, slot_of_row - SLOTS + 4 * part, -9).astype(F32)

    for part in range(3):
        wait_line(part)

    for half in range(2):
        for part in range(3):

            def select(j, carry, part=part, half=half):
                rows = slice(256 * half, 256 * half + 256)
                spread = nt(expand[part, rows, :], meta[part, j, 0:128, :])
                main = onehot(spread == slot_of_row[rows].astype(F32))
                extra = onehot(spread == extra_slot(part)[rows])
                chosen = jnp.concatenate([main, extra], axis=1)
                made = nn(chosen, gathered[part, j]).astype(BF16)
                if part == 1:
                    staged[1, 2 * half : 2 * half + 2, j // 2, :, j % 2] = made.reshape(
                        2, 2, 4, 16, COL
                    )
                else:
                    staged[part, 2 * half : 2 * half + 2, :, :, :, j] = made.reshape(
                        2, 2, 2, 2, 16, COL
                    )
                return carry

            lax.fori_loop(0, 4, select, 0)

        def send(k, carry):
            for part in range(3):
                dispatch_copy(part, k).start()
            return carry

        lax.fori_loop(1 if half == 0 else 16, 16 if half == 0 else 32, send, 0)
        if half == 0:
            for part in range(3):
                own_copy(part).start()

    def saved_copies(g, buffer):
        rows = pl.ds(pl.multiple_of(g * 16, 16), 16)
        return (
            pltpu.make_async_copy(gs_hbm.at[:, rows, :], gs_buf.at[buffer], gs_sem.at[0, buffer]),
            pltpu.make_async_copy(us_hbm.at[:, rows, :], us_buf.at[buffer], gs_sem.at[1, buffer]),
        )

    for copy in saved_copies(0, 0):
        copy.start()
    for copy in weight_copies():
        copy.wait()
    for part in range(3):
        own_copy(part).wait()

    def settle_dispatch(k, carry):
        for part in range(3):
            copy = dispatch_copy(part, k)
            copy.wait_send()
            a, dc, b = k // 8, (k // 4) % 2, (second[part] + k % 4) % 4
            pltpu.make_async_remote_copy(
                src_ref=message(staged, part, a, dc, b),
                dst_ref=message(landed, part, a, dc, b),
                send_sem=d_send.at[part, k],
                recv_sem=d_recv.at[part, a * 8 + dc * 4 + b],
                device_id=device(x, y, z, 1 - c),
                device_id_type=MESH,
            ).wait_recv()
        return carry

    lax.fori_loop(1, 32, settle_dispatch, 0)

    big = (256, 256)
    to_row, from_row = iota(big, 0), iota(big, 1)
    same_source = to_row // 16 == from_row // 16
    moves = [
        onehot(
            same_source
            & (from_row % 16 >= SLOTS)
            & (to_row % 16 == from_row % 16 - SLOTS + 4 * part)
        )
        for part in range(3)
    ]
    take = (256, 16 * SLOTS)
    by_source = onehot(
        (iota(take, 0) // 16 == iota(take, 1) % 16) & (iota(take, 0) % 16 == iota(take, 1) // 16)
    )
    diagonal = iota((128, 128), 0) == iota((128, 128), 1)

    def expert_group(g, carry):
        gx, gy = g // 2, g % 2
        buffer = g % 2

        @pl.when(g < 7)
        def _():
            for copy in saved_copies(g + 1, (g + 1) % 2):
                copy.start()

        for copy in saved_copies(g, buffer):
            copy.wait()
        rows = [landed[part, gx, gy].reshape(256, COL) for part in range(3)]
        last = (nn(moves[0], rows[0]) + nn(moves[1], rows[1]) + nn(moves[2], rows[2])).astype(BF16)
        projected = (
            nt(rows[0], wd[0]) + nt(rows[1], wd[1]) + nt(rows[2], wd[2]) + nt(last, wd[3])
        )
        gate = nn(by_source, gs_buf[buffer].reshape(16 * SLOTS, HID))
        up = nn(by_source, us_buf[buffer].reshape(16 * SLOTS, HID))
        sigmoid = jax.nn.sigmoid(gate)
        activated = gate * sigmoid
        up_grad = projected * activated
        inner = jnp.sum(up_grad * up, axis=1, keepdims=True)
        gate_grad = projected * up * sigmoid * (1.0 + gate * (1.0 - sigmoid))
        shape = (2, 2, 4, 16, HID)
        staged[0, gx, gy, :, :, :, :, 0:HID] = gate_grad.astype(BF16).reshape(shape)
        staged[1, gx, gy, :, :, :, :, 0:HID] = up_grad.astype(BF16).reshape(shape)
        for n in range(2):
            column = inner[128 * n : 128 * n + 128]
            line = jnp.sum(jnp.where(diagonal, column, 0.0), axis=0, keepdims=True)
            score_rows[pl.ds(g * 2 + n, 1), :] = line
        return carry

    lax.fori_loop(0, 8, expert_group, 0)

    score_send[...] = score_rows[...].astype(BF16)

    def plane_peer(k):
        to = plane_member(0, k // 8, (z + k % 4) % 4, here, (c + (k // 4) % 2) % 2)
        ids = device(*to)
        return ids, (ids[0] % 4) * 8 + ids[1]

    def score_copy(k):
        ids, _ = plane_peer(k)
        return pltpu.make_async_remote_copy(
            src_ref=score_send,
            dst_ref=score_plane.at[my_plane],
            send_sem=sp_send.at[k],
            recv_sem=sp_recv.at[my_plane],
            device_id=ids,
            device_id_type=MESH,
        )

    def start_score(k, carry):
        score_copy(k).start()
        return carry

    lax.fori_loop(1, 32, start_score, 0)
    score_plane[my_plane] = score_send[...]

    def return_copy(part, k):
        a, dc, b = k // 8, (k // 4) % 2, (second[part] + k % 4) % 4
        relay_core = (c + dc) % 2
        to = plane_member(part, 4 - (1 - 2 * relay_core) * a, b, here, relay_core)
        return pltpu.make_async_remote_copy(
            src_ref=message(landed, part, a, dc, b),
            dst_ref=message(back_hbm, part, a, dc, second[part]),
            send_sem=r_send.at[part, k],
            recv_sem=r_recv.at[part, a * 8 + dc * 4 + second[part]],
            device_id=device(*to),
            device_id_type=MESH,
        )

    def own_return(part):
        b = second[part]
        return pltpu.make_async_copy(
            message(landed, part, 0, 0, b), message(back_hbm, part, 0, 0, b), own_sem.at[part]
        )

    row_slot = iota((256, COL), 0) % 16

    def expert_unit(u, carry):
        a, dc = u // 2, u % 2
        relay_core = (c + dc) % 2
        ahead = 4 - (1 - 2 * relay_core) * a
        for part in range(3):
            place = (here[(part + 1) % 3] if part != 1 else z) + ahead
            if part == 0:
                ry = (y + ahead) % 4
                pair = [staged[n, :, ry // 2, relay_core, ry % 2, :, :, 0:HID] for n in range(2)]
            elif part == 1:
                rz = (z + ahead) % 4
                pair = [staged[n, :, :, relay_core, :, rz, :, 0:HID] for n in range(2)]
            else:
                rx = (x + ahead) % 4
                pair = [staged[n, rx, :, relay_core, :, :, :, 0:HID] for n in range(2)]
            gate_grad, up_grad = (v.reshape(256, HID) for v in pair)
            main = nt(gate_grad, wg[part * COL : (part + 1) * COL, :]) + nt(
                up_grad, wu[part * COL : (part + 1) * COL, :]
            )
            last = nt(gate_grad, wg[LAST:, :]) + nt(up_grad, wu[LAST:, :])
            made = jnp.where(
                row_slot < SLOTS, main, pltpu.roll(last, SLOTS - 4 * part, axis=0)
            ).astype(BF16)
            if part == 0:
                made = made.reshape(4, 4, 16, COL)
                for b in range(4):
                    landed[0, a, dc, b // 2, b % 2] = made[:, b]
            elif part == 1:
                made = made.reshape(4, 2, 2, 16, COL)
                for b in range(4):
                    landed[1, a, :, dc, :, b] = made[b]
            else:
                landed[2, a, dc] = made.reshape(2, 2, 4, 16, COL)

        def send(k, carry):
            for part in range(3):
                return_copy(part, k).start()
            return carry

        @pl.when(u == 0)
        def _():
            for part in range(3):
                own_return(part).start()

        lax.fori_loop(jnp.where(u == 0, 1, 4 * u), 4 * u + 4, send, 0)
        return carry

    lax.fori_loop(0, 8, expert_unit, 0)

    def settle_score(k, carry):
        score_copy(k).wait_send()
        ids, index = plane_peer(k)
        pltpu.make_async_remote_copy(
            src_ref=score_send,
            dst_ref=score_plane.at[index],
            send_sem=sp_send.at[k],
            recv_sem=sp_recv.at[index],
            device_id=ids,
            device_id_type=MESH,
        ).wait_recv()
        return carry

    lax.fori_loop(1, 32, settle_score, 0)
    plane_scores = score_plane[...].reshape(512, 128)
    for position in range(4):
        wanted = position * 4 + yh * 2 + c
        pickup = onehot(iota((32, 512), 1) == iota((32, 512), 0) * 16 + wanted)
        score_line[position] = nn(pickup, plane_scores).astype(BF16)

    def line_ids(step):
        return device((x + step) % 4, y, z, c)

    def line_score_copy(step):
        return pltpu.make_async_remote_copy(
            src_ref=score_line.at[(x + step) % 4],
            dst_ref=score_all.at[x],
            send_sem=sl_send.at[step],
            recv_sem=sl_recv.at[x],
            device_id=line_ids(step),
            device_id_type=MESH,
        )

    for step in (1, 2, 3):
        line_score_copy(step).start()
    score_all[x] = score_line[x]
    for step in (1, 2, 3):
        position = (x + step) % 4
        line_score_copy(step).wait_send()
        pltpu.make_async_remote_copy(
            src_ref=score_line.at[position],
            dst_ref=score_all.at[position],
            send_sem=sl_send.at[step],
            recv_sem=sl_recv.at[position],
            device_id=line_ids(step),
            device_id_type=MESH,
        ).wait_recv()

    mine = onehot(iota((16, 128), 1) == iota((16, 128), 0) + seq * 16)
    by_slot = nt(mine, score_all[...].reshape(128, 128))
    slots = slots_ref[...]
    combine = combine_ref[...]
    score = jnp.zeros(square, F32)
    for n in range(SLOTS):
        score = score + jnp.where(slots == float(n), by_slot[n : n + 1, :], 0.0)
    weighted = combine * score
    logit_grad = (weighted - combine * jnp.sum(weighted, axis=1, keepdims=True)).astype(BF16)
    logit_grad_t = nt(onehot(iota(square, 0) == iota(square, 1)), logit_grad).astype(BF16)
    for n in range(4):
        terms = nn(logit_grad_t, h_ref[:, n * COL : (n + 1) * COL]).astype(BF16)
        for m in range(8):
            staged[2, m // 2, n // 2, n % 2, m % 2, 0] = terms[16 * m : 16 * m + 16]

    def terms_copy(step):
        return pltpu.make_async_remote_copy(
            src_ref=staged.at[2, (x + step) % 4, :, :, :, 0],
            dst_ref=terms_in.at[x],
            send_sem=t_send.at[step],
            recv_sem=t_recv.at[x],
            device_id=line_ids(step),
            device_id_type=MESH,
        )

    for step in (1, 2, 3):
        terms_copy(step).start()
    total = staged[2, x, :, :, :, 0].astype(F32)
    for step in (1, 2, 3):
        position = (x + step) % 4
        terms_copy(step).wait_send()
        pltpu.make_async_remote_copy(
            src_ref=staged.at[2, position, :, :, :, 0],
            dst_ref=terms_in.at[position],
            send_sem=t_send.at[step],
            recv_sem=t_recv.at[position],
            device_id=line_ids(step),
            device_id_type=MESH,
        ).wait_recv()
        total = total + terms_in[position].astype(F32)
    for n in range(8):
        for m in range(2):
            block = total[n // 4, (n // 2) % 2, m]
            rows_out[16 * m : 16 * m + 16, n, :] = block[:, 512 * (n % 2) : 512 * (n % 2) + 512]

    def rows_copy(k):
        ids, index = plane_peer(k)
        return pltpu.make_async_remote_copy(
            src_ref=rows_out.at[index],
            dst_ref=rows_in.at[my_plane],
            send_sem=q_send.at[k],
            recv_sem=q_recv.at[my_plane],
            device_id=ids,
            device_id_type=MESH,
        )

    def start_rows(k, carry):
        rows_copy(k).start()
        return carry

    lax.fori_loop(1, 32, start_rows, 0)
    rows_in[my_plane] = rows_out[my_plane]

    for part in range(3):
        own_return(part).wait()

    def settle_return(k, carry):
        for part in range(3):
            return_copy(part, k).wait_send()
            a, dc, b = k // 8, (k // 4) % 2, (second[part] + k % 4) % 4
            pltpu.make_async_remote_copy(
                src_ref=message(landed, part, a, dc, b),
                dst_ref=message(back_hbm, part, a, dc, b),
                send_sem=r_send.at[part, k],
                recv_sem=r_recv.at[part, a * 8 + dc * 4 + b],
                device_id=device(x, y, z, 1 - c),
                device_id_type=MESH,
            ).wait_recv()
        return carry

    lax.fori_loop(1, 32, settle_return, 0)

    def load_copy(part):
        return pltpu.make_async_copy(back_hbm.at[part], staged.at[part], load_sem.at[part])

    for part in range(3):
        load_copy(part).start()

    def line_slot(part, position):
        n = part * 4 + position
        return wd.at[n // 3, pl.ds(pl.multiple_of((n % 3) * 256, 256), 256)]

    def part_copy(part, step):
        position = (here[part] + step) % 4
        return pltpu.make_async_remote_copy(
            src_ref=gathered.at[part, position],
            dst_ref=line_slot(part, here[part]),
            send_sem=p_send.at[part, step],
            recv_sem=p_recv.at[part, here[part]],
            device_id=device(*line_member(part, position, here, c)),
            device_id_type=MESH,
        )

    for part in range(3):
        load_copy(part).wait()
        lane_slot = iota((128, 512), 1) % 16
        lane_extra = jnp.where(lane_slot >= SLOTS, lane_slot - SLOTS + 4 * part, -9).astype(F32)

        def gather_back(step, carry, part=part, lane_slot=lane_slot, lane_extra=lane_extra):
            j = (here[part] + step) % 4
            spread = nt(meta[part, j, 0:128, :], expand[part])
            weight = nt(meta[part, j, 128:256, :], expand[part])
            main = jnp.where(spread == lane_slot.astype(F32), weight, 0.0).astype(BF16)
            extra = jnp.where(spread == lane_extra, weight, 0.0).astype(BF16)
            if part == 1:
                rows = staged[1, :, j // 2, :, j % 2]
            else:
                rows = staged[part, :, :, :, :, j]
            rows = rows.reshape(512, COL)
            gathered[part, j, 0:128, :] = nn(main, rows).astype(BF16)
            gathered[part, j, 128:256, :] = nn(extra, rows).astype(BF16)

            @pl.when(step > 0)
            def _():
                part_copy(part, step).start()

            return carry

        lax.fori_loop(0, 4, gather_back, 0)

    routed = [nt(logit_grad, rw_ref[n * COL : (n + 1) * COL, :]) for n in range(4)]
    tail = routed[3]
    for part in range(3):
        head = routed[part] + gathered[part, here[part], 0:128, :].astype(F32)
        tail = tail + gathered[part, here[part], 128:256, :].astype(F32)
        for step in (1, 2, 3):
            position = (here[part] + step) % 4
            part_copy(part, step).wait_send()
            arrived = line_slot(part, position)
            pltpu.make_async_remote_copy(
                src_ref=gathered.at[part, position],
                dst_ref=arrived,
                send_sem=p_send.at[part, step],
                recv_sem=p_recv.at[part, position],
                device_id=device(*line_member(part, position, here, c)),
                device_id_type=MESH,
            ).wait_recv()
            head = head + arrived[0:128, :].astype(F32)
            tail = tail + arrived[128:256, :].astype(F32)
        out_ref[:, part * COL : (part + 1) * COL] = head.astype(BF16)
    out_ref[:, LAST:] = tail.astype(BF16)

    def settle_rows(k, carry):
        rows_copy(k).wait_send()
        ids, index = plane_peer(k)
        pltpu.make_async_remote_copy(
            src_ref=rows_out.at[index],
            dst_ref=rows_in.at[index],
            send_sem=q_send.at[k],
            recv_sem=q_recv.at[index],
            device_id=ids,
            device_id_type=MESH,
        ).wait_recv()
        return carry

    lax.fori_loop(1, 32, settle_rows, 0)
    router_ref[...] = jnp.sum(rows_in[...], axis=0)

    for part in range(3):
        for step in (1, 2, 3):
            for copy in token_copies(part, step):
                copy.wait_send()
            meta_copy(part, step).wait_send()


def shards(
    grad_out,
    moe_input,
    router_weight,
    routes,
    gate_saved,
    up_saved,
    expert_gate,
    expert_up,
    expert_down,
):
    dma = pltpu.SemaphoreType.DMA
    whole = pl.BlockSpec(memory_space=pltpu.VMEM)
    away = pl.BlockSpec(memory_space=pl.ANY)
    blocks = (3, 4, 2, 2, 2, 4, 16, COL)
    input_grad, router_grad, _ = pl.pallas_call(
        kernel,
        out_shape=(
            jax.ShapeDtypeStruct((128, 4096), BF16),
            jax.ShapeDtypeStruct((8, 512), F32),
            jax.ShapeDtypeStruct(blocks, BF16),
        ),
        in_specs=[whole] * 4 + [away] * 5,
        out_specs=(whole, whole, away),
        scratch_shapes=[
            pltpu.VMEM((3, 4, 256, COL), BF16),
            pltpu.VMEM((3, 4, 256, 128), BF16),
            pltpu.VMEM(blocks, BF16),
            pltpu.VMEM(blocks, BF16),
            pltpu.VMEM((4, HID, COL), BF16),
            pltpu.VMEM((4096, HID), BF16),
            pltpu.VMEM((4096, HID), BF16),
            pltpu.VMEM((2, SLOTS, 16, HID), BF16),
            pltpu.VMEM((2, SLOTS, 16, HID), BF16),
            pltpu.VMEM((3, 512, 128), BF16),
            pltpu.VMEM((128, 128), F32),
            pltpu.VMEM((128, 128), F32),
            pltpu.VMEM((16, 128), F32),
            pltpu.VMEM((16, 128), BF16),
            pltpu.VMEM((32, 16, 128), BF16),
            pltpu.VMEM((4, 32, 128), BF16),
            pltpu.VMEM((4, 32, 128), BF16),
            pltpu.VMEM((4, 2, 2, 2, 16, COL), BF16),
            pltpu.VMEM((32, 8, 512), F32),
            pltpu.VMEM((32, 8, 512), F32),
            dma((6,)),
            dma((2, 2)),
            dma((3, 4, 2)),
            dma((3, 4, 2)),
            dma((3, 4)),
            dma((3, 4)),
            dma((3,)),
            dma((3, 32)),
            dma((3, 32)),
            dma((3, 32)),
            dma((3, 32)),
            dma((32,)),
            dma((32,)),
            dma((4,)),
            dma((4,)),
            dma((4,)),
            dma((4,)),
            dma((32,)),
            dma((32,)),
            dma((3,)),
            dma((3, 4)),
            dma((3, 4)),
        ],
        compiler_params=pltpu.CompilerParams(
            collective_id=0, has_side_effects=True, vmem_limit_bytes=62 << 20
        ),
        cost_estimate=pl.CostEstimate(
            flops=80_000_000_000, bytes_accessed=60 << 20, transcendentals=2 << 20
        ),
    )(
        grad_out,
        moe_input,
        router_weight,
        routes.T,
        jnp.transpose(gate_saved[0], (1, 0, 2)),
        jnp.transpose(up_saved[0], (1, 0, 2)),
        expert_gate[0],
        expert_up[0],
        expert_down[0],
    )
    return (input_grad, router_grad.reshape(1, 4096))


def solution(mesh):
    placed = (
        P(("dp", "seq"), None),
        P(("dp", "seq"), None),
        P(),
        P(("dp", "seq"), None),
        P(("dp", "seq"), None, None, None),
        P(("dp", "seq"), None, None, None),
        P(("dp", "seq"), None, None),
        P(("dp", "seq"), None, None),
        P(("dp", "seq"), None, None),
    )
    return jax.shard_map(
        shards,
        mesh=mesh,
        in_specs=placed,
        out_specs=(P(("dp", "seq"), None), P(("dp", "seq"), None)),
        check_vma=False,
    )
```

time: 838 us -> 348 us (0.42); the launches traced: 826 us -> 346 us
  waiting for transfers between devices: 526 us -> 0 us
  Pallas kernels: 0 us -> 342 us
  local copies, waits for them, and re-layouts: 161 us -> 3.63 us
  matrix products: 70.8 us -> 0 us
  starting transfers between devices: 28.1 us -> 0 us
  blocking collectives: 13.9 us -> 0 us
  between operations: 14.4 us -> 0.64 us
  other arithmetic: 12.2 us -> 0 us
    pallas_call x0 -> x1, Pallas kernels: none -> 342 us  [shards(): pl.pallas_call(kernel, out_shape=(jax.ShapeDtypeStruct((128, 4096), BF16)...]
    unnamed x2 -> x0, waiting for transfers between devices: 327 us -> none
    all_to_all x3 -> x0, waiting for transfers between devices: 199 us -> none  [the longest x1 189 us: shards(): lax.all_to_all(outgoing, ('dp', 'seq'), split_axis=0, concat_axis=0, tile...]
    reshape x5 -> x0, local copies, waits for them, and re-layouts: 72.1 us -> none  [the longest x1 18.2 us: shards(): pick_rows = arrived.reshape(experts * capacity, model_width)[position]]
    dot_general x6 -> x0, matrix products: 70.8 us -> none  [the longest x1 24 us: expert_backward(): lax.dot_general(gate_grad, gate_weight, (((1,), (1,)), ((), ())), preferr...]
    gather x3 -> x0, local copies, waits for them, and re-layouts: 37.6 us -> none  [the longest x1 21.3 us: shards(): pick_rows = arrived.reshape(experts * capacity, model_width)[position]]
    convert_element_type x10 -> x0, local copies, waits for them, and re-layouts: 34.9 us -> none  [the longest x3 16.9 us: expert_backward(): gate_value = gate_pre.astype(jnp.float32)]
    all_to_all x3 -> x0, starting transfers between devices: 27.9 us -> none  [the longest x1 12.3 us: shards(): lax.all_to_all(outgoing, ('dp', 'seq'), split_axis=0, concat_axis=0, tile...]
  transfers between devices with their start and end apart: 4 -> 0, of which waited for: 3 -> 0; matrix products, arithmetic and copies ran while one was open for 5% -> 0% of each run, Pallas kernels for 0% -> 0%
where the time goes in v1:
time: 348 us; the launch traced here: 346 us
  Pallas kernels  342 us (98%)
  local copies, waits for them, and re-layouts  3.63 us (1%)
    pallas_call x1, Pallas kernels, shards(): pl.pallas_call(kernel, out_shape=(jax.ShapeDtypeStruct((128, 4096), BF16)...  342 us

profile of v1, /device:TPU:1, one launch (start us, length us, event | category | flops | bytes accessed | tf_op | source)
XLA Modules:
  0.0 346.0 jit_solution(13351898245586084448)
XLA Ops:
  0.6 341.7 %shard_map.104 = (bf16[128,4096]{1,0:T(8,128)(2,1)}, f32[8,512]{1,0:T(8,128)}, bf16[3,4,2,2,2,4,16,1024]{7,6,5,4,3,2,1,0:T(8,128)(2,1)}) custom-call(bf16[128,4096]{1,0:T(8,128)(2,1)} %x_ref.1, bf16[128,4096]{1,0:T(8,128)(2,1)} %h_ref.1, bf16[4096,128]{1,0:T(8,128)(2,1)} %rw_ref.1, s32[8,128]{1,0:T(8,128)} %bitcast.20, bf16[12,128,768]{2,1,0:T(8,128)(2,1)} %bitcast.18, ...), custom_call_target="tpu_custom_call" | custom-call | flops 80000000000 | bytes 62914560 | tf_op jit(solution)/shard_map/pallas_call | solution.py:682
  342.3 1.3 copy.11
  343.7 2.3 copy.13

commit v2 on v1

--- a/solution.py
+++ b/solution.py
@@ -169,15 +169,19 @@
     b = (row // 16) % 4
     for part in range(3):
         owner = expert_id(*plane_member(part, ahead, b, here, core))
-        expand[part] = onehot(owner == lane)
+        expand[part] = onehot(owner == lane).reshape(4, 2, 64, 128)
 
     def message(buffer, part, a, dc, b):
         if part == 1:
             return buffer.at[1, a, :, dc, :, b]
         return buffer.at[part, a, dc, b // 2, b % 2]
 
+    def dispatch_place(part, k):
+        mixed = (k % 16) * 7 % 16
+        return mixed // 4, k // 16, (second[part] + sign * (mixed % 4) + 4) % 4
+
     def dispatch_copy(part, k):
-        a, dc, b = k // 8, (k // 4) % 2, (second[part] + k % 4) % 4
+        a, dc, b = dispatch_place(part, k)
         to = plane_member(part, sign * a + 4, b, here, (c + dc) % 2)
         landing = (
             landed.at[0, :, yh, c, yl, z],
@@ -203,7 +207,7 @@
             message(staged, part, 0, 0, second[part]), landing, own_sem.at[part]
         )
 
-    slot_of_row = iota((512, 128), 0) % 16
+    slot_of_row = iota((256, 128), 0) % 16
 
     def wait_line(part):
         for step in (1, 2, 3):
@@ -232,24 +236,19 @@
     for part in range(3):
         wait_line(part)
 
-    for half in range(2):
-        for part in range(3):
-
-            def select(j, carry, part=part, half=half):
-                rows = slice(256 * half, 256 * half + 256)
-                spread = nt(expand[part, rows, :], meta[part, j, 0:128, :])
-                main = onehot(spread == slot_of_row[rows].astype(F32))
-                extra = onehot(spread == extra_slot(part)[rows])
+    for dc in range(2):
+        for part in range(3):
+
+            def select(j, carry, part=part, dc=dc):
+                spread = nt(expand[part, :, dc].reshape(256, 128), meta[part, j, 0:128, :])
+                main = onehot(spread == slot_of_row.astype(F32))
+                extra = onehot(spread == extra_slot(part))
                 chosen = jnp.concatenate([main, extra], axis=1)
                 made = nn(chosen, gathered[part, j]).astype(BF16)
                 if part == 1:
-                    staged[1, 2 * half : 2 * half + 2, j // 2, :, j % 2] = made.reshape(
-                        2, 2, 4, 16, COL
-                    )
+                    staged[1, :, j // 2, dc, j % 2] = made.reshape(4, 4, 16, COL)
                 else:
-                    staged[part, 2 * half : 2 * half + 2, :, :, :, j] = made.reshape(
-                        2, 2, 2, 2, 16, COL
-                    )
+                    staged[part, :, dc, :, :, j] = made.reshape(4, 2, 2, 16, COL)
                 return carry
 
             lax.fori_loop(0, 4, select, 0)
@@ -259,13 +258,13 @@
                 dispatch_copy(part, k).start()
             return carry
 
-        lax.fori_loop(1 if half == 0 else 16, 16 if half == 0 else 32, send, 0)
-        if half == 0:
+        lax.fori_loop(1 if dc == 0 else 16, 16 if dc == 0 else 32, send, 0)
+        if dc == 0:
             for part in range(3):
                 own_copy(part).start()
 
     def saved_copies(g, buffer):
-        rows = pl.ds(pl.multiple_of(g * 16, 16), 16)
+        rows = pl.ds(pl.multiple_of(g % 4 * 32, 32), 32)
         return (
             pltpu.make_async_copy(gs_hbm.at[:, rows, :], gs_buf.at[buffer], gs_sem.at[0, buffer]),
             pltpu.make_async_copy(us_hbm.at[:, rows, :], us_buf.at[buffer], gs_sem.at[1, buffer]),
@@ -280,9 +279,7 @@
 
     def settle_dispatch(k, carry):
         for part in range(3):
-            copy = dispatch_copy(part, k)
-            copy.wait_send()
-            a, dc, b = k // 8, (k // 4) % 2, (second[part] + k % 4) % 4
+            a, dc, b = dispatch_place(part, k)
             pltpu.make_async_remote_copy(
                 src_ref=message(staged, part, a, dc, b),
                 dst_ref=message(landed, part, a, dc, b),
@@ -293,7 +290,10 @@
             ).wait_recv()
         return carry
 
-    lax.fori_loop(1, 32, settle_dispatch, 0)
+    def settle_send(k, carry):
+        for part in range(3):
+            dispatch_copy(part, k).wait_send()
+        return carry
 
     big = (256, 256)
     to_row, from_row = iota(big, 0), iota(big, 1)
@@ -306,14 +306,15 @@
         )
         for part in range(3)
     ]
-    take = (256, 16 * SLOTS)
-    by_source = onehot(
-        (iota(take, 0) // 16 == iota(take, 1) % 16) & (iota(take, 0) % 16 == iota(take, 1) // 16)
-    )
+    take = (256, 32 * SLOTS)
+    take_row, take_from = iota(take, 0), iota(take, 1)
+    source_row = take_row // 128 * 16 + take_row // 16 % 8
+    same_slot = take_row % 16 == take_from // 32
     diagonal = iota((128, 128), 0) == iota((128, 128), 1)
 
     def expert_group(g, carry):
-        gx, gy = g // 2, g % 2
+        gx = g % 4
+        core = jnp.where(g < 4, c, 1 - c)
         buffer = g % 2
 
         @pl.when(g < 7)
@@ -323,28 +324,32 @@
 
         for copy in saved_copies(g, buffer):
             copy.wait()
-        rows = [landed[part, gx, gy].reshape(256, COL) for part in range(3)]
+        rows = [landed[part, gx, :, core].reshape(256, COL) for part in range(3)]
         last = (nn(moves[0], rows[0]) + nn(moves[1], rows[1]) + nn(moves[2], rows[2])).astype(BF16)
         projected = (
             nt(rows[0], wd[0]) + nt(rows[1], wd[1]) + nt(rows[2], wd[2]) + nt(last, wd[3])
         )
-        gate = nn(by_source, gs_buf[buffer].reshape(16 * SLOTS, HID))
-        up = nn(by_source, us_buf[buffer].reshape(16 * SLOTS, HID))
+        by_source = onehot(same_slot & (take_from % 32 == source_row + 8 * core))
+        gate = nn(by_source, gs_buf[buffer].reshape(32 * SLOTS, HID))
+        up = nn(by_source, us_buf[buffer].reshape(32 * SLOTS, HID))
         sigmoid = jax.nn.sigmoid(gate)
         activated = gate * sigmoid
         up_grad = projected * activated
         inner = jnp.sum(up_grad * up, axis=1, keepdims=True)
         gate_grad = projected * up * sigmoid * (1.0 + gate * (1.0 - sigmoid))
         shape = (2, 2, 4, 16, HID)
-        staged[0, gx, gy, :, :, :, :, 0:HID] = gate_grad.astype(BF16).reshape(shape)
-        staged[1, gx, gy, :, :, :, :, 0:HID] = up_grad.astype(BF16).reshape(shape)
+        landed[0, gx, :, core, :, :, :, 0:HID] = gate_grad.astype(BF16).reshape(shape)
+        landed[1, gx, :, core, :, :, :, 0:HID] = up_grad.astype(BF16).reshape(shape)
         for n in range(2):
             column = inner[128 * n : 128 * n + 128]
             line = jnp.sum(jnp.where(diagonal, column, 0.0), axis=0, keepdims=True)
-            score_rows[pl.ds(g * 2 + n, 1), :] = line
-        return carry
-
-    lax.fori_loop(0, 8, expert_group, 0)
+            score_rows[pl.ds(gx * 4 + n * 2 + core, 1), :] = line
+        return carry
+
+    lax.fori_loop(1, 16, settle_dispatch, 0)
+    lax.fori_loop(0, 4, expert_group, 0)
+    lax.fori_loop(16, 32, settle_dispatch, 0)
+    lax.fori_loop(4, 8, expert_group, 0)
 
     score_send[...] = score_rows[...].astype(BF16)
 
@@ -371,23 +376,27 @@
     lax.fori_loop(1, 32, start_score, 0)
     score_plane[my_plane] = score_send[...]
 
+    def return_place(part, k):
+        a, dc = k // 8, (k // 4) % 2
+        relay_core = (c + dc) % 2
+        turn = 1 - 2 * relay_core
+        return a, dc, (second[part] + turn * (k % 4) + 4) % 4, relay_core, 4 - turn * a
+
     def return_copy(part, k):
-        a, dc, b = k // 8, (k // 4) % 2, (second[part] + k % 4) % 4
-        relay_core = (c + dc) % 2
-        to = plane_member(part, 4 - (1 - 2 * relay_core) * a, b, here, relay_core)
+        a, dc, b, relay_core, ahead = return_place(part, k)
         return pltpu.make_async_remote_copy(
-            src_ref=message(landed, part, a, dc, b),
+            src_ref=message(staged, part, a, dc, b),
             dst_ref=message(back_hbm, part, a, dc, second[part]),
             send_sem=r_send.at[part, k],
             recv_sem=r_recv.at[part, a * 8 + dc * 4 + second[part]],
-            device_id=device(*to),
+            device_id=device(*plane_member(part, ahead, b, here, relay_core)),
             device_id_type=MESH,
         )
 
     def own_return(part):
         b = second[part]
         return pltpu.make_async_copy(
-            message(landed, part, 0, 0, b), message(back_hbm, part, 0, 0, b), own_sem.at[part]
+            message(staged, part, 0, 0, b), message(back_hbm, part, 0, 0, b), own_sem.at[part]
         )
 
     row_slot = iota((256, COL), 0) % 16
@@ -397,16 +406,15 @@
         relay_core = (c + dc) % 2
         ahead = 4 - (1 - 2 * relay_core) * a
         for part in range(3):
-            place = (here[(part + 1) % 3] if part != 1 else z) + ahead
             if part == 0:
                 ry = (y + ahead) % 4
-                pair = [staged[n, :, ry // 2, relay_core, ry % 2, :, :, 0:HID] for n in range(2)]
+                pair = [landed[n, :, ry // 2, relay_core, ry % 2, :, :, 0:HID] for n in range(2)]
             elif part == 1:
                 rz = (z + ahead) % 4
-                pair = [staged[n, :, :, relay_core, :, rz, :, 0:HID] for n in range(2)]
+                pair = [landed[n, :, :, relay_core, :, rz, :, 0:HID] for n in range(2)]
             else:
                 rx = (x + ahead) % 4
-                pair = [staged[n, rx, :, relay_core, :, :, :, 0:HID] for n in range(2)]
+                pair = [landed[n, rx, :, relay_core, :, :, :, 0:HID] for n in range(2)]
             gate_grad, up_grad = (v.reshape(256, HID) for v in pair)
             main = nt(gate_grad, wg[part * COL : (part + 1) * COL, :]) + nt(
                 up_grad, wu[part * COL : (part + 1) * COL, :]
@@ -418,28 +426,27 @@
             if part == 0:
                 made = made.reshape(4, 4, 16, COL)
                 for b in range(4):
-                    landed[0, a, dc, b // 2, b % 2] = made[:, b]
+                    staged[0, a, dc, b // 2, b % 2] = made[:, b]
             elif part == 1:
                 made = made.reshape(4, 2, 2, 16, COL)
                 for b in range(4):
-                    landed[1, a, :, dc, :, b] = made[b]
+                    staged[1, a, :, dc, :, b] = made[b]
             else:
-                landed[2, a, dc] = made.reshape(2, 2, 4, 16, COL)
-
-        def send(k, carry):
-            for part in range(3):
+                staged[2, a, dc] = made.reshape(2, 2, 4, 16, COL)
+
+            @pl.when(u == 0)
+            def _(part=part):
+                own_return(part).start()
+
+            def send(k, carry, part=part):
                 return_copy(part, k).start()
-            return carry
-
-        @pl.when(u == 0)
-        def _():
-            for part in range(3):
-                own_return(part).start()
-
-        lax.fori_loop(jnp.where(u == 0, 1, 4 * u), 4 * u + 4, send, 0)
-        return carry
-
-    lax.fori_loop(0, 8, expert_unit, 0)
+                return carry
+
+            lax.fori_loop(jnp.where(u == 0, 1, 4 * u), 4 * u + 4, send, 0)
+        return carry
+
+    lax.fori_loop(1, 32, settle_send, 0)
+    lax.fori_loop(0, 4, expert_unit, 0)
 
     def settle_score(k, carry):
         score_copy(k).wait_send()
@@ -477,6 +484,9 @@
     for step in (1, 2, 3):
         line_score_copy(step).start()
     score_all[x] = score_line[x]
+
+    lax.fori_loop(4, 6, expert_unit, 0)
+
     for step in (1, 2, 3):
         position = (x + step) % 4
         line_score_copy(step).wait_send()
@@ -502,11 +512,11 @@
     for n in range(4):
         terms = nn(logit_grad_t, h_ref[:, n * COL : (n + 1) * COL]).astype(BF16)
         for m in range(8):
-            staged[2, m // 2, n // 2, n % 2, m % 2, 0] = terms[16 * m : 16 * m + 16]
+            landed[2, m // 2, n // 2, n % 2, m % 2, 0] = terms[16 * m : 16 * m + 16]
 
     def terms_copy(step):
         return pltpu.make_async_remote_copy(
-            src_ref=staged.at[2, (x + step) % 4, :, :, :, 0],
+            src_ref=landed.at[2, (x + step) % 4, :, :, :, 0],
             dst_ref=terms_in.at[x],
             send_sem=t_send.at[step],
             recv_sem=t_recv.at[x],
@@ -516,12 +526,13 @@
 
     for step in (1, 2, 3):
         terms_copy(step).start()
-    total = staged[2, x, :, :, :, 0].astype(F32)
+    lax.fori_loop(6, 8, expert_unit, 0)
+    total = landed[2, x, :, :, :, 0].astype(F32)
     for step in (1, 2, 3):
         position = (x + step) % 4
         terms_copy(step).wait_send()
         pltpu.make_async_remote_copy(
-            src_ref=staged.at[2, position, :, :, :, 0],
+            src_ref=landed.at[2, position, :, :, :, 0],
             dst_ref=terms_in.at[position],
             send_sem=t_send.at[step],
             recv_sem=t_recv.at[position],
@@ -552,15 +563,30 @@
     lax.fori_loop(1, 32, start_rows, 0)
     rows_in[my_plane] = rows_out[my_plane]
 
+    lane_slot = iota((128, 512), 1) % 16
+    for part in range(3):
+        lane_extra = jnp.where(lane_slot >= SLOTS, lane_slot - SLOTS + 4 * part, -9)
+
+        def weigh(j, carry, part=part, lane_extra=lane_extra):
+            rows_of = expand[part].reshape(512, 128)
+            spread = nt(meta[part, j, 0:128, :], rows_of)
+            weight = nt(meta[part, j, 128:256, :], rows_of)
+            main = jnp.where(spread == lane_slot.astype(F32), weight, 0.0).astype(BF16)
+            extra = jnp.where(spread == lane_extra.astype(F32), weight, 0.0).astype(BF16)
+            gathered[part, j, 0:128, 0:512] = main
+            gathered[part, j, 128:256, 0:512] = extra
+            return carry
+
+        lax.fori_loop(0, 4, weigh, 0)
+
     for part in range(3):
         own_return(part).wait()
 
     def settle_return(k, carry):
         for part in range(3):
-            return_copy(part, k).wait_send()
-            a, dc, b = k // 8, (k // 4) % 2, (second[part] + k % 4) % 4
+            a, dc, b, _, _ = return_place(part, k)
             pltpu.make_async_remote_copy(
-                src_ref=message(landed, part, a, dc, b),
+                src_ref=message(staged, part, a, dc, b),
                 dst_ref=message(back_hbm, part, a, dc, b),
                 send_sem=r_send.at[part, k],
                 recv_sem=r_recv.at[part, a * 8 + dc * 4 + b],
@@ -569,13 +595,15 @@
             ).wait_recv()
         return carry
 
-    lax.fori_loop(1, 32, settle_return, 0)
-
-    def load_copy(part):
-        return pltpu.make_async_copy(back_hbm.at[part], staged.at[part], load_sem.at[part])
-
-    for part in range(3):
-        load_copy(part).start()
+    def load_copy(part, a):
+        return pltpu.make_async_copy(
+            back_hbm.at[part, a], landed.at[part, a], load_sem.at[part, a]
+        )
+
+    for a in range(4):
+        lax.fori_loop(max(1, 8 * a), 8 * a + 8, settle_return, 0)
+        for part in range(3):
+            load_copy(part, a).start()
 
     def line_slot(part, position):
         n = part * 4 + position
@@ -592,32 +620,31 @@
             device_id_type=MESH,
         )
 
-    for part in range(3):
-        load_copy(part).wait()
-        lane_slot = iota((128, 512), 1) % 16
-        lane_extra = jnp.where(lane_slot >= SLOTS, lane_slot - SLOTS + 4 * part, -9).astype(F32)
-
-        def gather_back(step, carry, part=part, lane_slot=lane_slot, lane_extra=lane_extra):
-            j = (here[part] + step) % 4
-            spread = nt(meta[part, j, 0:128, :], expand[part])
-            weight = nt(meta[part, j, 128:256, :], expand[part])
-            main = jnp.where(spread == lane_slot.astype(F32), weight, 0.0).astype(BF16)
-            extra = jnp.where(spread == lane_extra, weight, 0.0).astype(BF16)
-            if part == 1:
-                rows = staged[1, :, j // 2, :, j % 2]
-            else:
-                rows = staged[part, :, :, :, :, j]
-            rows = rows.reshape(512, COL)
-            gathered[part, j, 0:128, :] = nn(main, rows).astype(BF16)
-            gathered[part, j, 128:256, :] = nn(extra, rows).astype(BF16)
-
-            @pl.when(step > 0)
-            def _():
-                part_copy(part, step).start()
-
-            return carry
-
-        lax.fori_loop(0, 4, gather_back, 0)
+    def gather_back(part, step):
+        j = (here[part] + step) % 4
+        if part == 1:
+            rows = landed[1, :, j // 2, :, j % 2]
+        else:
+            rows = landed[part, :, :, :, :, j]
+        weights = gathered[part, j, :, 0:512]
+        gathered[part, j] = nn(weights, rows.reshape(512, COL)).astype(BF16)
+
+    for part in range(3):
+        for a in range(4):
+            load_copy(part, a).wait()
+    for step in (2, 1, 3):
+        for part in range(3):
+            gather_back(part, step)
+            part_copy(part, step).start()
+    for part in range(3):
+        gather_back(part, 0)
+
+    def settle_return_send(k, carry):
+        for part in range(3):
+            return_copy(part, k).wait_send()
+        return carry
+
+    lax.fori_loop(1, 32, settle_return_send, 0)
 
     routed = [nt(logit_grad, rw_ref[n * COL : (n + 1) * COL, :]) for n in range(4)]
     tail = routed[3]
@@ -696,9 +723,9 @@
             pltpu.VMEM((4, HID, COL), BF16),
             pltpu.VMEM((4096, HID), BF16),
             pltpu.VMEM((4096, HID), BF16),
-            pltpu.VMEM((2, SLOTS, 16, HID), BF16),
-            pltpu.VMEM((2, SLOTS, 16, HID), BF16),
-            pltpu.VMEM((3, 512, 128), BF16),
+            pltpu.VMEM((2, SLOTS, 32, HID), BF16),
+            pltpu.VMEM((2, SLOTS, 32, HID), BF16),
+            pltpu.VMEM((3, 4, 2, 64, 128), BF16),
             pltpu.VMEM((128, 128), F32),
             pltpu.VMEM((128, 128), F32),
             pltpu.VMEM((16, 128), F32),
@@ -728,12 +755,12 @@
             dma((4,)),
             dma((32,)),
             dma((32,)),
-            dma((3,)),
+            dma((3, 4)),
             dma((3, 4)),
             dma((3, 4)),
         ],
         compiler_params=pltpu.CompilerParams(
-            collective_id=0, has_side_effects=True, vmem_limit_bytes=62 << 20
+            collective_id=0, has_side_effects=True, vmem_limit_bytes=63 << 20
         ),
         cost_estimate=pl.CostEstimate(
             flops=80_000_000_000, bytes_accessed=60 << 20, transcendentals=2 << 20

time: 348 us -> 314 us (0.902)
  Pallas kernels: 342 us -> 310 us
    pallas_call x1, Pallas kernels: 342 us -> 310 us  [shards(): pl.pallas_call(kernel, out_shape=(jax.ShapeDtypeStruct((128, 4096), BF16)...]
where the time goes in v2:
time: 314 us
  Pallas kernels  310 us (99%)
  local copies, waits for them, and re-layouts  3.63 us (1%)
    pallas_call x1, Pallas kernels, shards(): pl.pallas_call(kernel, out_shape=(jax.ShapeDtypeStruct((128, 4096), BF16)...  310 us

profile of v2, /device:TPU:1, one launch (start us, length us, event | category | flops | bytes accessed | tf_op | source)
XLA Modules:
  0.0 313.9 jit_solution(187380479938336976)
XLA Ops:
  0.6 309.6 %shard_map.104 = (bf16[128,4096]{1,0:T(8,128)(2,1)}, f32[8,512]{1,0:T(8,128)}, bf16[3,4,2,2,2,4,16,1024]{7,6,5,4,3,2,1,0:T(8,128)(2,1)}) custom-call(bf16[128,4096]{1,0:T(8,128)(2,1)} %x_ref.1, bf16[128,4096]{1,0:T(8,128)(2,1)} %h_ref.1, bf16[4096,128]{1,0:T(8,128)(2,1)} %rw_ref.1, s32[8,128]{1,0:T(8,128)} %bitcast.20, bf16[12,128,768]{2,1,0:T(8,128)(2,1)} %bitcast.18, ...), custom_call_target="tpu_custom_call" | custom-call | flops 80000000000 | bytes 62914560 | tf_op jit(solution)/shard_map/pallas_call | solution.py:709
  310.2 1.3 copy.11
  311.6 2.3 copy.13
